TPU v7x, 32 devices: a whole 2x2x4 slice. The times are simulated.
32 devices in a mesh: groups: 2 (over x), context: 8 (over z, y), tensor: 2 (over core).
Axes of the slice: x: 2, y: 2, z: 4, core: 2. Of those that a mesh axis runs over, the one named last changes fastest.
Arguments:
- queries: bfloat16 [8192, 2048], P(('groups', 'context'), 'tensor'), parts along dimension 0, may hold values from -60 to 60
- keys: bfloat16 [8192, 1024], P(('groups', 'context'), 'tensor'), parts along dimension 0, may hold values from -6 to 6
- values: bfloat16 [8192, 1024], P(('groups', 'context'), 'tensor'), parts along dimension 0, may hold values from -6 to 6
Outputs:
- attended: bfloat16 [8192, 2048], P(('groups', 'context', 'tensor')), parts along dimension 0
There are 2 independent parts, one for each index of `groups`. A program takes and returns all parts, laid end to end along the dimension named above; each array names one. Nothing has to cross between parts.
All inputs are finite; a program needn't handle non-finite values.
Results may differ from a plain program's by a relative error of at most 0.0049.
Values may be sent and summed in bfloat16 or wider, within the bound.
A program may use at most 64 MiB of HBM per device.

v0:
```python
import math

import jax
import jax.numpy as jnp
from jax import lax
from jax.sharding import PartitionSpec as P

HEAD_DIM = 128
WINDOW = 2048


cap_value = 50.0
query_scale = 144.0 ** (-0.5)


def passed_along(value, axis, steps):
    count = lax.axis_size(axis)
    initial, last = (max(0, -steps), min(count, count - steps))
    return lax.ppermute(value, axis, [(source, source + steps) for source in range(initial, last)])


def attend(state_pair, query_blocks, key_rows, value_rows, offsets, key_base):
    tok_rows, kv_heads, group_size, head_size = query_blocks.shape
    key_count = key_rows.shape[0]
    slice_len = math.gcd(key_count, max(512, tok_rows))
    slices = key_count // slice_len
    key_slices = key_rows.reshape(slices, slice_len, kv_heads, head_size)
    value_slices = value_rows.reshape(slices, slice_len, kv_heads, head_size)
    offset_slices = offsets.reshape(slices, slice_len)
    query_pos = jnp.arange(tok_rows, dtype=jnp.int32)

    def one_slice(inner_state, slice_parts):
        key_part, value_part, offset_part = slice_parts
        allowed = (
            (offset_part[None, :] <= query_pos[:, None])
            & (offset_part[None, :] > query_pos[:, None] - WINDOW)
            & (key_base + offset_part >= 0)[None, :]
        )

        def add_terms(state_in):
            weighted, totals = state_in
            scores = (
                jnp.einsum(
                    "tkgd,ukd->tkgu", query_blocks, key_part, preferred_element_type=jnp.float32
                )
                * query_scale
            )
            capped = cap_value * jnp.tanh(scores / cap_value)
            exp_terms = jnp.where(
                allowed[:, None, None, :], jnp.exp(capped), jnp.zeros_like(capped)
            )
            totals = totals + jnp.sum(exp_terms, axis=-1)
            weighted = weighted + jnp.einsum(
                "tkgu,ukd->tkgd",
                exp_terms.astype(jnp.bfloat16),
                value_part,
                preferred_element_type=jnp.float32,
            )
            return (weighted, totals)

        def keep_state(state_in):
            return state_in

        return (lax.cond(jnp.any(allowed), add_terms, keep_state, inner_state), None)

    new_state, unused = lax.scan(one_slice, state_pair, (key_slices, value_slices, offset_slices))
    return new_state


def local(queries, keys, values):
    tok_rows = queries.shape[0]
    kv_heads = keys.shape[1] // HEAD_DIM
    group_size = queries.shape[1] // keys.shape[1]
    block_span = WINDOW // tok_rows
    key_base = lax.axis_index("context") * tok_rows
    query_blocks = queries.reshape(tok_rows, kv_heads, group_size, HEAD_DIM)
    local_offsets = jnp.arange(tok_rows, dtype=jnp.int32)
    state_pair = (
        jnp.zeros((tok_rows, kv_heads, group_size, HEAD_DIM), jnp.float32),
        jnp.zeros((tok_rows, kv_heads, group_size), jnp.float32),
    )

    def fold_keys(current, key_rows, value_rows, offsets):
        key_view = key_rows.reshape(key_rows.shape[0], kv_heads, HEAD_DIM)
        value_view = value_rows.reshape(value_rows.shape[0], kv_heads, HEAD_DIM)
        return attend(current, query_blocks, key_view, value_view, offsets, key_base)

    state_pair = fold_keys(state_pair, keys, values, local_offsets)
    held_keys, held_values = (keys, values)
    for level_bit in range(block_span.bit_length() - 1):
        reach = 1 << level_bit
        arrived_keys, arrived_values = passed_along((held_keys, held_values), "context", reach)
        offsets = jnp.arange(reach * tok_rows, dtype=jnp.int32) - (2 * reach - 1) * tok_rows
        state_pair = fold_keys(state_pair, arrived_keys, arrived_values, offsets)
        held_keys = jnp.concatenate([arrived_keys, held_keys], axis=0)
        held_values = jnp.concatenate([arrived_values, held_values], axis=0)
    far_keys, far_values = passed_along((keys, values), "context", block_span)
    state_pair = fold_keys(state_pair, far_keys, far_values, local_offsets - block_span * tok_rows)
    weighted, totals = state_pair
    head_output = (
        (weighted / totals[..., None]).astype(jnp.bfloat16).reshape(tok_rows, queries.shape[1])
    )
    return lax.all_to_all(head_output, "tensor", split_axis=0, concat_axis=1, tiled=True)


def solution(mesh):
    return jax.shard_map(
        local,
        mesh=mesh,
        in_specs=(
            P(("groups", "context"), "tensor"),
            P(("groups", "context"), "tensor"),
            P(("groups", "context"), "tensor"),
        ),
        out_specs=P(("groups", "context", "tensor"), None),
        check_vma=False,
    )
```

profile of v0, /device:TPU:21, one launch (start us, length us, event | category | flops | bytes accessed | tf_op | source)
XLA Modules:
  0.0 142.1 jit_solution(4806463903761569047)
XLA Ops:
  0.0 3.1 %collective-permute-start = (bf16[512,512]{1,0:T(8,128)(2,1)}, bf16[512,512]{1,0:T(8,128)(2,1)S(1)}, u32[]{:S(2)}, u32[]{:S(2)}) collective-permute-start(bf16[512,512]{1,0:T(8,128)(2,1)} %param.14), channel_id=1, source_target_pairs={{0,2},{2,4},{4,6},{6,8},{8,10},{10,12},{12,14},{1,3},{3,5},{5,7},{... | collective-permute-start | bytes 1572872 | tf_op jit(solution)/shard_map/ppermute | solution.py:19
  3.1 3.1 %collective-permute-start.1 = (bf16[512,512]{1,0:T(8,128)(2,1)}, bf16[512,512]{1,0:T(8,128)(2,1)S(1)}, u32[]{:S(2)}, u32[]{:S(2)}) collective-permute-start(bf16[512,512]{1,0:T(8,128)(2,1)} %param.15), channel_id=1, source_target_pairs={{0,2},{2,4},{4,6},{6,8},{8,10},{10,12},{12,14},{1,3},{3,5},{5,7},{... | collective-permute-start | bytes 1572872 | tf_op jit(solution)/shard_map/ppermute | solution.py:19
  6.3 8.6 %collective-permute-done = bf16[512,512]{1,0:T(8,128)(2,1)S(1)} collective-permute-done((bf16[512,512]{1,0:T(8,128)(2,1)}, bf16[512,512]{1,0:T(8,128)(2,1)S(1)}, u32[]{:S(2)}, u32[]{:S(2)}) %collective-permute-start) | collective-permute-done | bytes 524320 | tf_op jit(solution)/shard_map/ppermute | solution.py:19
  17.2 3.2 %collective-permute-start.2 = (bf16[1024,512]{1,0:T(8,128)(2,1)}, bf16[1024,512]{1,0:T(8,128)(2,1)}, u32[]{:S(2)}, u32[]{:S(2)}) collective-permute-start(bf16[1024,512]{1,0:T(8,128)(2,1)} %pad_maximum_fusion), channel_id=1, source_target_pairs={{0,4},{2,6},{4,8},{6,10},{8,12},{10,14},{1,5},{3,7},{5,9},{7,11},{... | collective-permute-start | bytes 3145736 | tf_op jit(solution)/shard_map/ppermute | solution.py:19
  20.4 5.8 %collective-permute-done.1 = bf16[512,512]{1,0:T(8,128)(2,1)S(1)} collective-permute-done((bf16[512,512]{1,0:T(8,128)(2,1)}, bf16[512,512]{1,0:T(8,128)(2,1)S(1)}, u32[]{:S(2)}, u32[]{:S(2)}) %collective-permute-start.1) | collective-permute-done | bytes 524320 | tf_op jit(solution)/shard_map/ppermute | solution.py:19
  28.4 3.2 %collective-permute-start.3 = (bf16[1024,512]{1,0:T(8,128)(2,1)}, bf16[1024,512]{1,0:T(8,128)(2,1)}, u32[]{:S(2)}, u32[]{:S(2)}) collective-permute-start(bf16[1024,512]{1,0:T(8,128)(2,1)} %pad_maximum_fusion.1), channel_id=1, source_target_pairs={{0,4},{2,6},{4,8},{6,10},{8,12},{10,14},{1,5},{3,7},{5,9},{7,11},{... | collective-permute-start | bytes 3145736 | tf_op jit(solution)/shard_map/ppermute | solution.py:19
  39.8 2.5 %fusion.67 = (pred[]{:T(512)}, pred[]{:T(512)}, pred[]{:T(512)}, pred[512,512]{0,1:T(8,128)(4,1)S(1)}, pred[512,512]{0,1:T(8,128)(4,1)}, /*index=5*/pred[512,512]{0,1:T(8,128)(4,1)}) fusion(pred[512]{0:T(512)(128)(4,1)S(1)} %get-tuple-element.487, s32[512]{0:T(512)S(1)} %get-tuple-element.490, pred[512]{0:T(512)(128)(4,1)S(1)} %get-tuple-element.488, ...), kind=kLoop, calls=%fused_computation.79 | loop fusion | flops 3932157 | bytes 792067 | tf_op jit(solution)/shard_map/while/body/eval_jaxpr/reduce_or | solution.py:64
  45.7 7.6 %conditional.4 = ((f32[512,4,2,128]{3,0,2,1:T(8,128)S(1)}, f32[512,4,2]{0,2,1:T(2,128)S(1)})) conditional(s32[]{:T(128)} %convert_element_type.37, (f32[512,4,2,128]{3,0,2,1:T(8,128)S(1)}, f32[512,4,2]{0,2,1:T(2,128)S(1)}) %tuple.56, (pred[512,512]{0,1:T(8,128)(4,1)}, bf16[512,4,128]{0,2,1:T(8,128)(2,1)}, bf16[512,4,2,128]{0,3,2,1:T(8,128)(2,1)S(1)}, ...), branch_computations={%region_3.4_spmd, %region_4.0_spmd} | conditional | flops 1091043328 | bytes 26804304 | solution.py:64
  45.7 4.2 %fusion.2 = (f32[512,4,2]{0,2,1:T(2,128)S(1)}, f32[4,512,512,2]{2,1,3,0:T(8,128)S(1)}) fusion(pred[512,512]{0,1:T(8,128)(4,1)} %get-tuple-element.304, bf16[512,4,2,128]{0,3,2,1:T(8,128)(2,1)S(1)} %get-tuple-element.429, bf16[512,4,128]{0,2,1:T(8,128)(2,1)} %get-tuple-element.428), kind=kOutput, calls=%fused_computation.2 | convolution fusion | flops 545255424 | bytes 10240000 | tf_op jit(solution)/shard_map/while/body/eval_jaxpr/cond/branch_1_fun/tkgd,ukd->tkgu/dot_general | solution.py:43
  49.9 3.3 %bitcast_add_fusion = f32[512,4,2,128]{3,0,2,1:T(8,128)S(1)} fusion(f32[512,4,2,128]{3,0,2,1:T(8,128)S(1)} %get-tuple-element.303, f32[4,512,512,2]{2,1,3,0:T(8,128)S(1)} %get-tuple-element.475, pred[512,512]{0,1:T(8,128)(4,1)S(1)} %copy-done.5, bf16[512,4,128]{0,2,1:T(8,128)(2,1)S(1)} %copy-done.3), kind=kOutput, calls=%fused_computation.6 | convolution fusion | flops 545783808 | bytes 13369344 | tf_op jit(solution)/shard_map/while/body/eval_jaxpr/cond/branch_1_fun/tkgu,ukd->tkgd/dot_general | solution.py:53
  53.2 15.4 %conditional.5 = ((f32[512,4,2,128]{3,0,2,1:T(8,128)S(1)}, f32[512,4,2]{0,2,1:T(2,128)S(1)})) conditional(s32[]{:T(128)} %convert_element_type.36, (f32[512,4,2,128]{3,0,2,1:T(8,128)S(1)}, f32[512,4,2]{0,2,1:T(2,128)S(1)}) %get-tuple-element.595, (pred[512,512]{0,1:T(8,128)(4,1)S(1)}, bf16[512,512]{1,0:T(8,128)(2,1)}, ...), branch_computations={%region_6.7_spmd, %region_7.9_spmd} | conditional | flops 1091043328 | bytes 25755672 | solution.py:64
  55.2 5.8 %fusion.15 = (f32[512,4,2]{0,2,1:T(2,128)S(1)}, f32[4,512,512,2]{2,1,3,0:T(8,128)}) fusion(pred[512,512]{0,1:T(8,128)(4,1)S(1)} %get-tuple-element.310, bf16[512,4,2,128]{0,3,2,1:T(8,128)(2,1)S(1)} %get-tuple-element.435, bf16[512,4,128,1]{2,1,0,3:T(4,128)(2,1)} %bitcast.94), kind=kOutput, calls=%fused_computation.14 | convolution fusion | flops 545255424 | bytes 10240000 | tf_op jit(solution)/shard_map/while/body/eval_jaxpr/cond/branch_1_fun/tkgd,ukd->tkgu/dot_general | solution.py:43
  63.0 5.4 %bitcast_add_fusion.1 = f32[512,4,2,128]{3,0,2,1:T(8,128)S(1)} fusion(f32[512,4,2,128]{3,0,2,1:T(8,128)S(1)} %get-tuple-element.309, f32[4,512,512,2]{2,1,3,0:T(8,128)} %get-tuple-element.477, pred[512,512]{0,1:T(8,128)(4,1)S(1)} %get-tuple-element.310, bf16[512,4,128,1]{2,1,0,3:T(4,128)(2,1)} %bitcast.95), kind=kOutput, calls=%fused_computation.18 | convolution fusion | flops 545783808 | bytes 13369344 | tf_op jit(solution)/shard_map/while/body/eval_jaxpr/cond/branch_1_fun/tkgu,ukd->tkgd/dot_general | solution.py:53
  77.6 18.1 %while.11 = (s32[]{:T(128)}, f32[512,4,2,128]{3,0,2,1:T(8,128)S(1)}, f32[512,4,2]{0,2,1:T(2,128)S(1)}, s32[2,512]{1,0:T(2,128)S(1)}, s32[]{:T(128)}, /*index=5*/...) while((s32[]{:T(128)}, ...), condition=%wide.region_14.15_spmd.clone.clone, body=%wide.region_9.14_spmd.clone.clone.sunk | while | flops 1092355584 | bytes 28126956 | solution.py:66
  79.3 7.4 %conditional.10 = ((f32[512,4,2,128]{3,0,2,1:T(8,128)S(1)}, f32[512,4,2]{0,2,1:T(2,128)S(1)})) conditional(s32[]{:T(128)} %convert_element_type.59, (f32[512,4,2,128]{3,0,2,1:T(8,128)S(1)}, f32[512,4,2]{0,2,1:T(2,128)S(1)}) %tuple.107, (pred[512,512]{0,1:T(8,128)(4,1)S(1)}, bf16[2,512,4,128]{3,1,2,0:T(8,128)(2,1)}, s32[]{:T(128)}, ...), branch_computations={%region_11.11_spmd, %region_12.13_spmd} | conditional | flops 1091043328 | bytes 27853368 | solution.py:64
  79.3 4.1 %fusion.28 = (f32[512,4,2]{0,2,1:T(2,128)S(1)}, f32[4,512,512,2]{2,1,3,0:T(8,128)S(1)}) fusion(pred[512,512]{0,1:T(8,128)(4,1)S(1)} %get-tuple-element.316, bf16[512,4,2,128]{3,0,2,1:T(8,128)(2,1)} %get-tuple-element.319, bf16[2,512,4,128]{3,1,2,0:T(8,128)(2,1)} %get-tuple-element.317, s32[]{:T(128)} %get-tuple-element.318), kind=kOutput, calls=%fused_computation.26 | convolution fusion | flops 545255424 | bytes 10240512 | tf_op jit(solution)/shard_map/while/body/eval_jaxpr/cond/branch_1_fun/tkgd,ukd->tkgu/dot_general | solution.py:43
  83.4 3.2 %bitcast_add_fusion.2 = f32[512,4,2,128]{3,0,2,1:T(8,128)S(1)} fusion(f32[512,4,2,128]{3,0,2,1:T(8,128)S(1)} %get-tuple-element.315, f32[4,512,512,2]{2,1,3,0:T(8,128)S(1)} %get-tuple-element.479, pred[512,512]{0,1:T(8,128)(4,1)S(1)} %get-tuple-element.316, bf16[2,512,4,128]{3,1,2,0:T(8,128)(2,1)S(1)} %copy-done.2, s32[]{:T(128)} %get-tuple-element.318), kind=kOutput, calls=%fused_computation.30 | convolution fusion | flops 545783808 | bytes 13369348 | tf_op jit(solution)/shard_map/while/body/eval_jaxpr/cond/branch_1_fun/tkgu,ukd->tkgd/dot_general | solution.py:53
  88.4 7.4 %conditional.10 = ((f32[512,4,2,128]{3,0,2,1:T(8,128)S(1)}, f32[512,4,2]{0,2,1:T(2,128)S(1)})) conditional(s32[]{:T(128)} %convert_element_type.59, (f32[512,4,2,128]{3,0,2,1:T(8,128)S(1)}, f32[512,4,2]{0,2,1:T(2,128)S(1)}) %tuple.107, (pred[512,512]{0,1:T(8,128)(4,1)S(1)}, bf16[2,512,4,128]{3,1,2,0:T(8,128)(2,1)}, s32[]{:T(128)}, ...), branch_computations={%region_11.11_spmd, %region_12.13_spmd} | conditional | flops 1091043328 | bytes 27853368 | solution.py:64
  88.4 4.1 %fusion.28 = (f32[512,4,2]{0,2,1:T(2,128)S(1)}, f32[4,512,512,2]{2,1,3,0:T(8,128)S(1)}) fusion(pred[512,512]{0,1:T(8,128)(4,1)S(1)} %get-tuple-element.316, bf16[512,4,2,128]{3,0,2,1:T(8,128)(2,1)} %get-tuple-element.319, bf16[2,512,4,128]{3,1,2,0:T(8,128)(2,1)} %get-tuple-element.317, s32[]{:T(128)} %get-tuple-element.318), kind=kOutput, calls=%fused_computation.26 | convolution fusion | flops 545255424 | bytes 10240512 | tf_op jit(solution)/shard_map/while/body/eval_jaxpr/cond/branch_1_fun/tkgd,ukd->tkgu/dot_general | solution.py:43
  92.5 3.2 %bitcast_add_fusion.2 = f32[512,4,2,128]{3,0,2,1:T(8,128)S(1)} fusion(f32[512,4,2,128]{3,0,2,1:T(8,128)S(1)} %get-tuple-element.315, f32[4,512,512,2]{2,1,3,0:T(8,128)S(1)} %get-tuple-element.479, pred[512,512]{0,1:T(8,128)(4,1)S(1)} %get-tuple-element.316, bf16[2,512,4,128]{3,1,2,0:T(8,128)(2,1)S(1)} %copy-done.2, s32[]{:T(128)} %get-tuple-element.318), kind=kOutput, calls=%fused_computation.30 | convolution fusion | flops 545783808 | bytes 13369348 | tf_op jit(solution)/shard_map/while/body/eval_jaxpr/cond/branch_1_fun/tkgu,ukd->tkgd/dot_general | solution.py:53
  95.8 14.4 %conditional.6 = ((f32[512,4,2,128]{3,0,2,1:T(8,128)S(1)}, f32[512,4,2]{0,2,1:T(2,128)S(1)})) conditional(s32[]{:T(128)} %convert_element_type.35, (f32[512,4,2,128]{3,0,2,1:T(8,128)S(1)}, f32[512,4,2]{0,2,1:T(2,128)S(1)}) %tuple.60, (pred[512,512]{0,1:T(8,128)(4,1)}, bf16[512,512]{1,0:T(8,128)(2,1)}, bf16[512,4,2,128]{0,3,2,1:T(8,128)(2,1)S(1)}, ...), branch_computations={%region_15.16_spmd, %region_16.18_spmd} | conditional | flops 1091043328 | bytes 26804276 | solution.py:64
  97.8 5.9 %fusion.45 = (f32[512,4,2]{0,2,1:T(2,128)S(1)}, f32[4,512,512,2]{2,1,3,0:T(8,128)}) fusion(pred[512,512]{0,1:T(8,128)(4,1)} %get-tuple-element.336, bf16[512,4,2,128]{0,3,2,1:T(8,128)(2,1)S(1)} %get-tuple-element.449, bf16[512,4,128,1]{2,1,0,3:T(4,128)(2,1)} %bitcast.96), kind=kOutput, calls=%fused_computation.42 | convolution fusion | flops 545255424 | bytes 10240000 | tf_op jit(solution)/shard_map/while/body/eval_jaxpr/cond/branch_1_fun/tkgd,ukd->tkgu/dot_general | solution.py:43
  104.8 5.3 %bitcast_add_fusion.3 = f32[512,4,2,128]{3,0,2,1:T(8,128)S(1)} fusion(f32[512,4,2,128]{3,0,2,1:T(8,128)S(1)} %get-tuple-element.335, f32[4,512,512,2]{2,1,3,0:T(8,128)} %get-tuple-element.481, pred[512,512]{0,1:T(8,128)(4,1)S(1)} %copy-done.4, bf16[512,4,128,1]{2,1,0,3:T(4,128)(2,1)S(1)} %bitcast.97), kind=kOutput, calls=%fused_computation.46 | convolution fusion | flops 545783808 | bytes 13369344 | tf_op jit(solution)/shard_map/while/body/eval_jaxpr/cond/branch_1_fun/tkgu,ukd->tkgd/dot_general | solution.py:53
  112.7 27.4 %all_to_all.19 = bf16[2,256,1024]{2,1,0:T(8,128)(2,1)S(1)} all-to-all(bf16[2,256,1024]{2,1,0:T(8,128)(2,1)S(1)} %all_to_all.14), channel_id=1, replica_groups=mesh['groups'=2,'context'=8,'tensor'=2] {'tensor'}, dimensions={0} | all-to-all | bytes 2097152 | tf_op jit(solution)/shard_map/all_to_all | solution.py:103
  (56 shorter events, 36.9 us)
Async XLA Ops:
  0.0 14.9 %collective-permute-start = (bf16[512,512]{1,0:T(8,128)(2,1)}, bf16[512,512]{1,0:T(8,128)(2,1)S(1)}, u32[]{:S(2)}, u32[]{:S(2)}) collective-permute-start(bf16[512,512]{1,0:T(8,128)(2,1)} %param.14), channel_id=1, source_target_pairs={{0,2},{2,4},{4,6},{6,8},{8,10},{10,12},{12,14},{1,3},{3,5},{5,7},{... | collective-permute-start | bytes 1572872 | tf_op jit(solution)/shard_map/ppermute | solution.py:19
  3.1 23.0 %collective-permute-start.1 = (bf16[512,512]{1,0:T(8,128)(2,1)}, bf16[512,512]{1,0:T(8,128)(2,1)S(1)}, u32[]{:S(2)}, u32[]{:S(2)}) collective-permute-start(bf16[512,512]{1,0:T(8,128)(2,1)} %param.15), channel_id=1, source_target_pairs={{0,2},{2,4},{4,6},{6,8},{8,10},{10,12},{12,14},{1,3},{3,5},{5,7},{... | collective-permute-start | bytes 1572872 | tf_op jit(solution)/shard_map/ppermute | solution.py:19
  14.9 23.4 %copy-start = (bf16[512,512]{1,0:T(8,128)(2,1)}, bf16[512,512]{1,0:T(8,128)(2,1)S(1)}, u32[]{:S(2)}) copy-start(bf16[512,512]{1,0:T(8,128)(2,1)S(1)} %collective-permute-done) | copy-start | bytes 1572868
  17.2 51.5 %collective-permute-start.2 = (bf16[1024,512]{1,0:T(8,128)(2,1)}, bf16[1024,512]{1,0:T(8,128)(2,1)}, u32[]{:S(2)}, u32[]{:S(2)}) collective-permute-start(bf16[1024,512]{1,0:T(8,128)(2,1)} %pad_maximum_fusion), channel_id=1, source_target_pairs={{0,4},{2,6},{4,8},{6,10},{8,12},{10,14},{1,5},{3,7},{5,9},{7,11},{... | collective-permute-start | bytes 3145736 | tf_op jit(solution)/shard_map/ppermute | solution.py:19
  26.1 12.2 %copy-start.1 = (bf16[512,512]{1,0:T(8,128)(2,1)}, bf16[512,512]{1,0:T(8,128)(2,1)S(1)}, u32[]{:S(2)}) copy-start(bf16[512,512]{1,0:T(8,128)(2,1)S(1)} %collective-permute-done.1) | copy-start | bytes 1572868
  28.4 44.7 %collective-permute-start.3 = (bf16[1024,512]{1,0:T(8,128)(2,1)}, bf16[1024,512]{1,0:T(8,128)(2,1)}, u32[]{:S(2)}, u32[]{:S(2)}) collective-permute-start(bf16[1024,512]{1,0:T(8,128)(2,1)} %pad_maximum_fusion.1), channel_id=1, source_target_pairs={{0,4},{2,6},{4,8},{6,10},{8,12},{10,14},{1,5},{3,7},{5,9},{7,11},{... | collective-permute-start | bytes 3145736 | tf_op jit(solution)/shard_map/ppermute | solution.py:19
  31.6 64.2 %collective-permute-start.4 = (bf16[512,512]{1,0:T(8,128)(2,1)}, bf16[512,512]{1,0:T(8,128)(2,1)}, u32[]{:S(2)}, u32[]{:S(2)}) collective-permute-start(bf16[512,512]{1,0:T(8,128)(2,1)} %param.14), channel_id=1, source_target_pairs={{0,8},{2,10},{4,12},{6,14},{1,9},{3,11},{5,13},{7,15},{16,24},{18,... | collective-permute-start | bytes 1572872 | tf_op jit(solution)/shard_map/ppermute | solution.py:19
  32.9 62.9 %collective-permute-start.5 = (bf16[512,512]{1,0:T(8,128)(2,1)}, bf16[512,512]{1,0:T(8,128)(2,1)}, u32[]{:S(2)}, u32[]{:S(2)}) collective-permute-start(bf16[512,512]{1,0:T(8,128)(2,1)} %param.15), channel_id=1, source_target_pairs={{0,8},{2,10},{4,12},{6,14},{1,9},{3,11},{5,13},{7,15},{16,24},{18,... | collective-permute-start | bytes 1572872 | tf_op jit(solution)/shard_map/ppermute | solution.py:19
  45.7 4.2 %copy-start.3 = (bf16[512,4,128]{0,2,1:T(8,128)(2,1)S(1)}, bf16[512,4,128]{0,2,1:T(8,128)(2,1)}, u32[]{:S(2)}) copy-start(bf16[512,4,128]{0,2,1:T(8,128)(2,1)} %get-tuple-element.430) | copy-start | bytes 1572868 | tf_op jit(solution)/shard_map/while/body/eval_jaxpr/cond
  45.7 4.2 %copy-start.5 = (pred[512,512]{0,1:T(8,128)(4,1)S(1)}, pred[512,512]{0,1:T(8,128)(4,1)}, u32[]{:S(2)}) copy-start(pred[512,512]{0,1:T(8,128)(4,1)} %get-tuple-element.304) | copy-start | bytes 786436 | tf_op jit(solution)/shard_map/while/body/eval_jaxpr/cond
  79.3 4.1 %copy-start.2 = (bf16[2,512,4,128]{3,1,2,0:T(8,128)(2,1)S(1)}, bf16[2,512,4,128]{3,1,2,0:T(8,128)(2,1)}, u32[]{:S(2)}) copy-start(bf16[2,512,4,128]{3,1,2,0:T(8,128)(2,1)} %get-tuple-element.320) | copy-start | bytes 3145732 | tf_op jit(solution)/shard_map/while/body/eval_jaxpr/cond
  88.4 4.1 %copy-start.2 = (bf16[2,512,4,128]{3,1,2,0:T(8,128)(2,1)S(1)}, bf16[2,512,4,128]{3,1,2,0:T(8,128)(2,1)}, u32[]{:S(2)}) copy-start(bf16[2,512,4,128]{3,1,2,0:T(8,128)(2,1)} %get-tuple-element.320) | copy-start | bytes 3145732 | tf_op jit(solution)/shard_map/while/body/eval_jaxpr/cond
  97.8 7.1 %copy-start.4 = (pred[512,512]{0,1:T(8,128)(4,1)S(1)}, pred[512,512]{0,1:T(8,128)(4,1)}, u32[]{:S(2)}) copy-start(pred[512,512]{0,1:T(8,128)(4,1)} %get-tuple-element.336) | copy-start | bytes 786436 | tf_op jit(solution)/shard_map/while/body/eval_jaxpr/cond
where the time goes:
time: 143 us; the launch traced here: 142 us
  matrix products  44.4 us (31%)
  blocking collectives  27.4 us (19%)
  local copies, waits for them, and re-layouts  26.9 us (19%)
  starting transfers between devices  15.3 us (11%)
  waiting for transfers between devices  14.4 us (10%)
  other arithmetic  9.86 us (7%)
  between operations  2.07 us (1%)
  loops' own time  1.77 us (1%)
    all_to_all x1, blocking collectives, local(): lax.all_to_all(head_output, 'tensor', split_axis=0, concat_axis=1, tiled=...  27.4 us
    dot_general x5, matrix products, add_terms(): jnp.einsum('tkgd,ukd->tkgu', query_blocks, key_part, preferred_element_ty...  24 us
    dot_general x5, matrix products, add_terms(): jnp.einsum('tkgu,ukd->tkgd', exp_terms.astype(jnp.bfloat16), value_part,...  20.4 us
    ppermute x6, starting transfers between devices, passed_along(): lax.ppermute(value, axis, [(source, source + steps) for source in range(i...  15.3 us
    ppermute x6, waiting for transfers between devices, passed_along(): lax.ppermute(value, axis, [(source, source + steps) for source in range(i...  14.4 us
    unnamed x10, local copies, waits for them, and re-layouts  11.7 us
    squeeze x4, local copies, waits for them, and re-layouts, attend(): lax.scan(one_slice, state_pair, (key_slices, value_slices, offset_slices))  7.08 us
  transfers between devices with their start and end apart: 6, of which 2 were waited for; matrix products, arithmetic and copies ran while one was open for 44% of the time, Pallas kernels for 0%

commit v1 on v0

v1 whole, which is shorter than its diff:
```python
import functools
import math

import jax
import jax.numpy as jnp
from jax import lax
from jax.experimental import pallas as pl
from jax.experimental.pallas import tpu as pltpu
from jax.sharding import PartitionSpec as P

HEAD_DIM = 128
WINDOW = 2048
SPAN = 4
MESH = pl.DeviceIdType.MESH

CAP = 50.0
SCORE_FACTOR = 144.0 ** (-0.5) / CAP
EXP_FACTOR = CAP * math.log2(math.e)


def kernel(
    blocks,
    q_ref,
    k_ref,
    v_ref,
    out_ref,
    held,
    acc,
    outgoing,
    up_own_send,
    up_relay_send,
    cross_send,
    recv_sem,
    out_send,
    out_recv,
):
    rows = q_ref.shape[0]
    half = rows // 2
    kv_heads = k_ref.shape[1] // HEAD_DIM
    own_cols = q_ref.shape[1]
    c = lax.axis_index("context")
    t = lax.axis_index("tensor")
    odd = lax.rem(c, 2)
    pair = c + 1 - 2 * odd
    other = 1 - t
    has_up = c + 2 < blocks
    has_down = c >= 2

    barrier = pltpu.get_barrier_semaphore()
    pl.semaphore_signal(barrier, inc=1, device_id={"context": pair}, device_id_type=MESH)
    pl.semaphore_signal(barrier, inc=1, device_id={"tensor": other}, device_id_type=MESH)

    @pl.when(has_up)
    def _():
        pl.semaphore_signal(barrier, inc=1, device_id={"context": c + 2}, device_id_type=MESH)

    @pl.when(has_down)
    def _():
        pl.semaphore_signal(barrier, inc=1, device_id={"context": c - 2}, device_id_type=MESH)

    pl.semaphore_wait(barrier, 2 + has_up.astype(jnp.int32) + has_down.astype(jnp.int32))

    def columns(head):
        return pl.ds(pl.multiple_of(head * HEAD_DIM, HEAD_DIM), HEAD_DIM)

    def source(slot, which, h):
        if slot == 0:
            return (k_ref, v_ref)[which].at[:, columns(h)]
        return held.at[slot - 1, which, h]

    def copy(slot, into, which, h, to, send):
        return pltpu.make_async_remote_copy(
            src_ref=source(slot, which, h),
            dst_ref=held.at[into - 1, which, h],
            send_sem=send,
            recv_sem=recv_sem.at[into - 1, which, h],
            device_id={"context": to},
            device_id_type=MESH,
        )

    def up_own(which, h):
        return copy(0, 2, which, h, c + 2, up_own_send.at[which, h])

    def up_relay(which, h):
        return copy(2, 4, which, h, c + 2, up_relay_send.at[which, h])

    def cross(slot, into, which, h):
        return copy(slot, into, which, h, pair, cross_send.at[(into - 1) // 2, which, h])

    @pl.loop(0, kv_heads)
    def _(h):
        for which in range(2):

            @pl.when(has_up)
            def _():
                up_own(which, h).start()

            @pl.when(odd == 0)
            def _():
                cross(0, 1, which, h).start()

    def landed(slot, which, h):
        copy(0, slot, which, h, pair, cross_send.at[0, which, h]).wait_recv()

    def terms(h, g, row_at, row_count, slot, key_at, key_count, mask):
        q = q_ref[pl.ds(row_at, row_count), columns(2 * h + g)]
        key_rows = source(slot, 0, h)[pl.ds(key_at, key_count), :]
        value_rows = source(slot, 1, h)[pl.ds(key_at, key_count), :]
        scores = lax.dot_general(
            q, key_rows, (((1,), (1,)), ((), ())), preferred_element_type=jnp.float32
        )
        exp_terms = jnp.exp2(EXP_FACTOR * jnp.tanh(scores * SCORE_FACTOR))
        if mask is not None:
            i = row_at + lax.broadcasted_iota(jnp.int32, exp_terms.shape, 0)
            j = key_at + lax.broadcasted_iota(jnp.int32, exp_terms.shape, 1)
            allowed = j <= i if mask == "own" else j > i
            exp_terms = jnp.where(allowed, exp_terms, jnp.zeros_like(exp_terms))
        beside = jnp.concatenate([value_rows, jnp.ones_like(value_rows)], axis=1)
        return jnp.dot(
            exp_terms.astype(jnp.bfloat16), beside, preferred_element_type=jnp.float32
        )

    def attend_own(h):
        @pl.loop(0, 2)
        def _(g):
            acc[2 * h + g, pl.ds(0, half), :] = terms(h, g, 0, half, 0, 0, half, "own")
            acc[2 * h + g, pl.ds(half, half), :] = terms(h, g, half, half, 0, 0, rows, "own")

    def attend_far(h):
        @pl.loop(0, 2)
        def _(g):
            acc[2 * h + g, pl.ds(0, half), :] += terms(h, g, 0, half, 4, 0, rows, "far")
            acc[2 * h + g, pl.ds(half, half), :] += terms(h, g, half, half, 4, half, half, "far")

    def attend_whole(h, slot):
        @pl.loop(0, 4)
        def _(step):
            g = step // 2
            row_at = pl.multiple_of(lax.rem(step, 2) * half, half)
            acc[2 * h + g, pl.ds(row_at, half), :] += terms(
                h, g, row_at, half, slot, 0, rows, None
            )

    def take_two(h):
        @pl.when(has_down)
        def _():
            for which in range(2):
                landed(2, which, h)

                @pl.when(has_up)
                def _():
                    up_relay(which, h).start()

                @pl.when(odd == 0)
                def _():
                    cross(2, 3, which, h).start()

                @pl.when(odd == 1)
                def _():
                    cross(2, 1, which, h).start()

            attend_whole(h, 2)

    def take_one(h):
        @pl.when(c >= 1)
        def _():
            for which in range(2):
                landed(1, which, h)
            attend_whole(h, 1)

    def take_four(h):
        @pl.when(c >= 4)
        def _():
            for which in range(2):
                landed(4, which, h)

                @pl.when(odd == 1)
                def _():
                    cross(4, 3, which, h).start()

            attend_far(h)

    def hand_over(h):
        col = pl.multiple_of(t * own_cols + h * 2 * HEAD_DIM, 2 * HEAD_DIM)
        return pltpu.make_async_remote_copy(
            src_ref=outgoing.at[h],
            dst_ref=out_ref.at[:, pl.ds(col, 2 * HEAD_DIM)],
            send_sem=out_send.at[h],
            recv_sem=out_recv.at[h],
            device_id={"tensor": other},
            device_id_type=MESH,
        )

    def take_three(h):
        @pl.when(c >= 3)
        def _():
            for which in range(2):
                landed(3, which, h)
            attend_whole(h, 3)

        def finished(g, owner):
            part = acc[2 * h + g, pl.ds(pl.multiple_of(owner * half, half), half), :]
            return (part[:, :HEAD_DIM] / part[:, HEAD_DIM:]).astype(out_ref.dtype)

        for g in range(2):
            outgoing[h, :, pl.ds(g * HEAD_DIM, HEAD_DIM)] = finished(g, other)
        hand_over(h).start()
        for g in range(2):
            col = pl.multiple_of(t * own_cols + (2 * h + g) * HEAD_DIM, HEAD_DIM)
            out_ref[:, pl.ds(col, HEAD_DIM)] = finished(g, t)

    last = kv_heads - 1

    @pl.loop(0, kv_heads)
    def _(h):
        attend_own(h)

    take_two(0)

    @pl.loop(0, last)
    def _(h):
        take_two(h + 1)
        take_one(h)

    take_four(0)
    take_one(last)

    @pl.loop(0, last)
    def _(h):
        take_four(h + 1)
        take_three(h)

    take_three(last)

    @pl.loop(0, kv_heads)
    def _(h):
        hand_over(h).wait()
        for which in range(2):

            @pl.when(has_up)
            def _():
                up_own(which, h).wait_send()

            @pl.when(has_up & has_down)
            def _():
                up_relay(which, h).wait_send()

            @pl.when((odd == 0) | (c >= 2))
            def _():
                cross(0, 1, which, h).wait_send()

            @pl.when(((odd == 0) & (c >= 2)) | (c >= 4))
            def _():
                cross(0, 3, which, h).wait_send()


def local(blocks, queries, keys, values):
    rows = queries.shape[0]
    kv_heads = keys.shape[1] // HEAD_DIM
    heads = queries.shape[1] // HEAD_DIM
    assert WINDOW == SPAN * rows and blocks % 2 == 0 and heads == 2 * kv_heads
    return pl.pallas_call(
        functools.partial(kernel, blocks),
        out_shape=jax.ShapeDtypeStruct((rows // 2, 2 * queries.shape[1]), queries.dtype),
        in_specs=[pl.BlockSpec(memory_space=pltpu.VMEM)] * 3,
        out_specs=pl.BlockSpec(memory_space=pltpu.VMEM),
        scratch_shapes=[
            pltpu.VMEM((SPAN, 2, kv_heads, rows, HEAD_DIM), keys.dtype),
            pltpu.VMEM((heads, rows, 2 * HEAD_DIM), jnp.float32),
            pltpu.VMEM((kv_heads, rows // 2, 2 * HEAD_DIM), queries.dtype),
            pltpu.SemaphoreType.DMA((2, kv_heads)),
            pltpu.SemaphoreType.DMA((2, kv_heads)),
            pltpu.SemaphoreType.DMA((2, 2, kv_heads)),
            pltpu.SemaphoreType.DMA((SPAN, 2, kv_heads)),
            pltpu.SemaphoreType.DMA((kv_heads,)),
            pltpu.SemaphoreType.DMA((kv_heads,)),
        ],
        compiler_params=pltpu.CompilerParams(
            collective_id=0, has_side_effects=True, vmem_limit_bytes=40 * 1024 * 1024
        ),
    )(queries, keys, values)


def solution(mesh):
    return jax.shard_map(
        functools.partial(local, mesh.shape["context"]),
        mesh=mesh,
        in_specs=(P(("groups", "context"), "tensor"),) * 3,
        out_specs=P(("groups", "context", "tensor"), None),
        check_vma=False,
    )
```

time: 143 us -> 61.4 us (0.43)
  the two profiles are of different devices: /device:TPU:21 before, /device:TPU:17 now
where the time goes in v1:
time: 61.4 us; the launch traced here: 61.2 us
  Pallas kernels  56.9 us (93%)
  local copies, waits for them, and re-layouts  4.28 us (7%)
    pallas_call x1, Pallas kernels, local(): pl.pallas_call(functools.partial(kernel, blocks), out_shape=jax.ShapeDtyp...  56.9 us
    unnamed x7, local copies, waits for them, and re-layouts  4.28 us

profile of v1, /device:TPU:17, one launch (start us, length us, event | category | flops | bytes accessed | tf_op | source)
XLA Modules:
  0.0 61.2 jit_solution(10186124667624322993)
XLA Ops:
  0.0 0.0 copy-start
  0.0 1.2 %copy-done = bf16[512,1024]{1,0:T(8,128)(2,1)S(1)} copy-done((bf16[512,1024]{1,0:T(8,128)(2,1)S(1)}, bf16[512,1024]{1,0:T(8,128)(2,1)}, u32[]{:S(2)}) %copy-start) | copy-done | bytes 1048600
  1.2 0.0 copy-start.1
  1.2 1.0 %copy-done.1 = bf16[512,512]{1,0:T(8,128)(2,1)S(1)} copy-done((bf16[512,512]{1,0:T(8,128)(2,1)S(1)}, bf16[512,512]{1,0:T(8,128)(2,1)}, u32[]{:S(2)}) %copy-start.1) | copy-done | bytes 524312
  2.3 0.0 copy-start.2
  2.3 1.0 %copy-done.2 = bf16[512,512]{1,0:T(8,128)(2,1)S(1)} copy-done((bf16[512,512]{1,0:T(8,128)(2,1)S(1)}, bf16[512,512]{1,0:T(8,128)(2,1)}, u32[]{:S(2)}) %copy-start.2) | copy-done | bytes 524312
  3.3 56.9 %shard_map.37 = bf16[256,2048]{1,0:T(8,128)(2,1)S(1)} custom-call(bf16[512,1024]{1,0:T(8,128)(2,1)S(1)} %copy-done, bf16[512,512]{1,0:T(8,128)(2,1)S(1)} %copy-done.1, bf16[512,512]{1,0:T(8,128)(2,1)S(1)} %copy-done.2), custom_call_target="tpu_custom_call" | custom-call | tf_op jit(solution)/shard_map/pallas_call | solution.py:262
  60.2 1.0 %copy.5 = bf16[256,2048]{1,0:T(8,128)(2,1)} copy(bf16[256,2048]{1,0:T(8,128)(2,1)S(1)} %shard_map.37) | data formatting | bytes 2097152
Async XLA Ops:
  0.0 1.2 %copy-start = (bf16[512,1024]{1,0:T(8,128)(2,1)S(1)}, bf16[512,1024]{1,0:T(8,128)(2,1)}, u32[]{:S(2)}) copy-start(bf16[512,1024]{1,0:T(8,128)(2,1)} %q_ref.1) | copy-start | bytes 3145732
  1.2 1.0 %copy-start.1 = (bf16[512,512]{1,0:T(8,128)(2,1)S(1)}, bf16[512,512]{1,0:T(8,128)(2,1)}, u32[]{:S(2)}) copy-start(bf16[512,512]{1,0:T(8,128)(2,1)} %k_ref.1) | copy-start | bytes 1572868
  2.3 1.0 %copy-start.2 = (bf16[512,512]{1,0:T(8,128)(2,1)S(1)}, bf16[512,512]{1,0:T(8,128)(2,1)}, u32[]{:S(2)}) copy-start(bf16[512,512]{1,0:T(8,128)(2,1)} %v_ref.1) | copy-start | bytes 1572868

commit v2 on v1

--- a/solution.py
+++ b/solution.py
@@ -20,19 +20,25 @@
 
 def kernel(
     blocks,
+    q_hbm,
+    k_hbm,
+    v_hbm,
+    out_ref,
     q_ref,
     k_ref,
     v_ref,
-    out_ref,
     held,
     acc,
     outgoing,
+    kept,
     up_own_send,
     up_relay_send,
     cross_send,
     recv_sem,
     out_send,
     out_recv,
+    fetch_sem,
+    keep_sem,
 ):
     rows = q_ref.shape[0]
     half = rows // 2
@@ -46,6 +52,13 @@
     has_up = c + 2 < blocks
     has_down = c >= 2
 
+    fetches = [
+        pltpu.make_async_copy(far, near, fetch_sem.at[at])
+        for at, (far, near) in enumerate(((q_hbm, q_ref), (k_hbm, k_ref), (v_hbm, v_ref)))
+    ]
+    for fetch in fetches:
+        fetch.start()
+
     barrier = pltpu.get_barrier_semaphore()
     pl.semaphore_signal(barrier, inc=1, device_id={"context": pair}, device_id_type=MESH)
     pl.semaphore_signal(barrier, inc=1, device_id={"tensor": other}, device_id_type=MESH)
@@ -70,7 +83,11 @@
 
     def copy(slot, into, which, h, to, send):
         return pltpu.make_async_remote_copy(
-            src_ref=source(slot, which, h),
+            src_ref=(
+                (k_hbm, v_hbm)[which].at[:, columns(h)]
+                if slot == 0
+                else held.at[slot - 1, which, h]
+            ),
             dst_ref=held.at[into - 1, which, h],
             send_sem=send,
             recv_sem=recv_sem.at[into - 1, which, h],
@@ -86,18 +103,6 @@
 
     def cross(slot, into, which, h):
         return copy(slot, into, which, h, pair, cross_send.at[(into - 1) // 2, which, h])
-
-    @pl.loop(0, kv_heads)
-    def _(h):
-        for which in range(2):
-
-            @pl.when(has_up)
-            def _():
-                up_own(which, h).start()
-
-            @pl.when(odd == 0)
-            def _():
-                cross(0, 1, which, h).start()
 
     def landed(slot, which, h):
         copy(0, slot, which, h, pair, cross_send.at[0, which, h]).wait_recv()
@@ -141,62 +146,81 @@
                 h, g, row_at, half, slot, 0, rows, None
             )
 
-    def take_two(h):
-        @pl.when(has_down)
-        def _():
-            for which in range(2):
-                landed(2, which, h)
-
-                @pl.when(has_up)
-                def _():
-                    up_relay(which, h).start()
-
-                @pl.when(odd == 0)
-                def _():
-                    cross(2, 3, which, h).start()
-
-                @pl.when(odd == 1)
-                def _():
-                    cross(2, 1, which, h).start()
-
-            attend_whole(h, 2)
-
-    def take_one(h):
-        @pl.when(c >= 1)
-        def _():
-            for which in range(2):
-                landed(1, which, h)
-            attend_whole(h, 1)
-
-    def take_four(h):
-        @pl.when(c >= 4)
-        def _():
-            for which in range(2):
-                landed(4, which, h)
-
-                @pl.when(odd == 1)
-                def _():
-                    cross(4, 3, which, h).start()
-
-            attend_far(h)
+    def send_own(h, which):
+        @pl.when(has_up)
+        def _():
+            up_own(which, h).start()
+
+        @pl.when(odd == 0)
+        def _():
+            cross(0, 1, which, h).start()
+
+    def sent_own(h, which):
+        @pl.when(has_up)
+        def _():
+            up_own(which, h).wait_send()
+
+        @pl.when(odd == 0)
+        def _():
+            cross(0, 1, which, h).wait_send()
+
+    def send_relay(h, which):
+        @pl.when(has_up & has_down)
+        def _():
+            up_relay(which, h).start()
+
+        @pl.when((odd == 0) & has_down)
+        def _():
+            cross(2, 3, which, h).start()
+
+    def sent_relay(h, which):
+        @pl.when(has_up & has_down)
+        def _():
+            up_relay(which, h).wait_send()
+
+        @pl.when((odd == 0) & has_down)
+        def _():
+            cross(2, 3, which, h).wait_send()
+
+    def take(slot, h, which):
+        @pl.when(c >= slot)
+        def _():
+            landed(slot, which, h)
+
+            @pl.when(odd == 1)
+            def _():
+                cross(slot, slot - 1, which, h).start()
+
+    def attend(slot, h):
+        @pl.when(c >= slot)
+        def _():
+            if slot % 2 == 1:
+                for which in range(2):
+                    landed(slot, which, h)
+            if slot == 4:
+                attend_far(h)
+            else:
+                attend_whole(h, slot)
+
+    def out_columns(h):
+        col = pl.multiple_of(t * own_cols + h * 2 * HEAD_DIM, 2 * HEAD_DIM)
+        return out_ref.at[:, pl.ds(col, 2 * HEAD_DIM)]
+
+    def keep(h):
+        return pltpu.make_async_copy(kept.at[h], out_columns(h), keep_sem.at[h])
 
     def hand_over(h):
-        col = pl.multiple_of(t * own_cols + h * 2 * HEAD_DIM, 2 * HEAD_DIM)
         return pltpu.make_async_remote_copy(
             src_ref=outgoing.at[h],
-            dst_ref=out_ref.at[:, pl.ds(col, 2 * HEAD_DIM)],
+            dst_ref=out_columns(h),
             send_sem=out_send.at[h],
             recv_sem=out_recv.at[h],
             device_id={"tensor": other},
             device_id_type=MESH,
         )
 
-    def take_three(h):
-        @pl.when(c >= 3)
-        def _():
-            for which in range(2):
-                landed(3, which, h)
-            attend_whole(h, 3)
+    def finish(h):
+        attend(3, h)
 
         def finished(g, owner):
             part = acc[2 * h + g, pl.ds(pl.multiple_of(owner * half, half), half), :]
@@ -206,52 +230,79 @@
             outgoing[h, :, pl.ds(g * HEAD_DIM, HEAD_DIM)] = finished(g, other)
         hand_over(h).start()
         for g in range(2):
-            col = pl.multiple_of(t * own_cols + (2 * h + g) * HEAD_DIM, HEAD_DIM)
-            out_ref[:, pl.ds(col, HEAD_DIM)] = finished(g, t)
+            kept[h, :, pl.ds(g * HEAD_DIM, HEAD_DIM)] = finished(g, t)
+        keep(h).start()
 
     last = kv_heads - 1
+    for which in range(2):
+        send_own(0, which)
+    for fetch in fetches:
+        fetch.wait()
+    attend_own(0)
+
+    @pl.loop(1, kv_heads)
+    def _(h):
+        sent_own(h - 1, 0)
+        send_own(h, 0)
+        take(2, h - 1, 0)
+        attend_own(h)
+        sent_own(h - 1, 1)
+        send_own(h, 1)
+        take(2, h - 1, 1)
+        attend(2, h - 1)
+
+        @pl.when(h >= 2)
+        def _():
+            attend(1, h - 2)
+
+    for which in range(2):
+        sent_own(last, which)
+        send_relay(0, which)
+        take(2, last, which)
+        if which == 0:
+            attend(1, last - 1)
+    attend(2, last)
+
+    for which in range(2):
+        sent_relay(0, which)
+        send_relay(1, which)
+        take(4, 0, which)
+        if which == 0:
+            attend(1, last)
+    attend(4, 0)
+
+    @pl.loop(2, kv_heads)
+    def _(h):
+        sent_relay(h - 1, 0)
+        send_relay(h, 0)
+        take(4, h - 1, 0)
+        finish(h - 2)
+        sent_relay(h - 1, 1)
+        send_relay(h, 1)
+        take(4, h - 1, 1)
+        attend(4, h - 1)
+
+    take(4, last, 0)
+    finish(last - 1)
+    take(4, last, 1)
+    attend(4, last)
+    finish(last)
+    for which in range(2):
+        sent_relay(last, which)
 
     @pl.loop(0, kv_heads)
     def _(h):
-        attend_own(h)
-
-    take_two(0)
-
-    @pl.loop(0, last)
-    def _(h):
-        take_two(h + 1)
-        take_one(h)
-
-    take_four(0)
-    take_one(last)
-
-    @pl.loop(0, last)
-    def _(h):
-        take_four(h + 1)
-        take_three(h)
-
-    take_three(last)
-
-    @pl.loop(0, kv_heads)
-    def _(h):
+        keep(h).wait()
         hand_over(h).wait()
         for which in range(2):
 
-            @pl.when(has_up)
+            @pl.when((odd == 1) & (c >= 2))
             def _():
-                up_own(which, h).wait_send()
-
-            @pl.when(has_up & has_down)
+                cross(2, 1, which, h).wait_send()
+
+            @pl.when((odd == 1) & (c >= 4))
             def _():
-                up_relay(which, h).wait_send()
-
-            @pl.when((odd == 0) | (c >= 2))
-            def _():
-                cross(0, 1, which, h).wait_send()
-
-            @pl.when(((odd == 0) & (c >= 2)) | (c >= 4))
-            def _():
-                cross(0, 3, which, h).wait_send()
+                cross(4, 3, which, h).wait_send()
 
 
 def local(blocks, queries, keys, values):
@@ -262,11 +313,15 @@
     return pl.pallas_call(
         functools.partial(kernel, blocks),
         out_shape=jax.ShapeDtypeStruct((rows // 2, 2 * queries.shape[1]), queries.dtype),
-        in_specs=[pl.BlockSpec(memory_space=pltpu.VMEM)] * 3,
-        out_specs=pl.BlockSpec(memory_space=pltpu.VMEM),
+        in_specs=[pl.BlockSpec(memory_space=pltpu.HBM)] * 3,
+        out_specs=pl.BlockSpec(memory_space=pltpu.HBM),
         scratch_shapes=[
+            pltpu.VMEM(queries.shape, queries.dtype),
+            pltpu.VMEM(keys.shape, keys.dtype),
+            pltpu.VMEM(values.shape, values.dtype),
             pltpu.VMEM((SPAN, 2, kv_heads, rows, HEAD_DIM), keys.dtype),
             pltpu.VMEM((heads, rows, 2 * HEAD_DIM), jnp.float32),
+            pltpu.VMEM((kv_heads, rows // 2, 2 * HEAD_DIM), queries.dtype),
             pltpu.VMEM((kv_heads, rows // 2, 2 * HEAD_DIM), queries.dtype),
             pltpu.SemaphoreType.DMA((2, kv_heads)),
             pltpu.SemaphoreType.DMA((2, kv_heads)),
@@ -274,9 +329,11 @@
             pltpu.SemaphoreType.DMA((SPAN, 2, kv_heads)),
             pltpu.SemaphoreType.DMA((kv_heads,)),
             pltpu.SemaphoreType.DMA((kv_heads,)),
+            pltpu.SemaphoreType.DMA((3,)),
+            pltpu.SemaphoreType.DMA((kv_heads,)),
         ],
         compiler_params=pltpu.CompilerParams(
-            collective_id=0, has_side_effects=True, vmem_limit_bytes=40 * 1024 * 1024
+            collective_id=0, has_side_effects=True, vmem_limit_bytes=56 * 1024 * 1024
         ),
     )(queries, keys, values)
 

time: 61.4 us -> 59.7 us (0.972)
  local copies, waits for them, and re-layouts: 4.28 us -> 2.3 us
    unnamed x7 -> x1, local copies, waits for them, and re-layouts: 4.28 us -> 2.3 us
where the time goes in v2:
time: 59.7 us; the launch traced here: 59.6 us
  Pallas kernels  57.3 us (96%)
  local copies, waits for them, and re-layouts  2.3 us (4%)
    pallas_call x1, Pallas kernels, local(): pl.pallas_call(functools.partial(kernel, blocks), out_shape=jax.ShapeDtyp...  57.3 us
    unnamed x1, local copies, waits for them, and re-layouts  2.3 us

profile of v2, /device:TPU:17, one launch (start us, length us, event | category | flops | bytes accessed | tf_op | source)
XLA Modules:
  0.0 59.6 jit_solution(7861467934221807939)
XLA Ops:
  0.0 57.3 %shard_map.37 = bf16[256,2048]{1,0:T(8,128)(2,1)} custom-call(bf16[512,1024]{1,0:T(8,128)(2,1)} %q_hbm.1, bf16[512,512]{1,0:T(8,128)(2,1)} %k_hbm.1, bf16[512,512]{1,0:T(8,128)(2,1)} %v_hbm.1), custom_call_target="tpu_custom_call" | custom-call | tf_op jit(solution)/shard_map/pallas_call | solution.py:313
  57.3 2.3 %copy.5 = bf16[256,2048]{1,0:T(8,128)(2,1)} copy(bf16[256,2048]{1,0:T(8,128)(2,1)} %shard_map.37) | data formatting | bytes 2097152

commit v3 on v2

--- a/solution.py
+++ b/solution.py
@@ -282,9 +282,9 @@
         take(4, h - 1, 1)
         attend(4, h - 1)
 
-    take(4, last, 0)
+    for which in range(2):
+        take(4, last, which)
     finish(last - 1)
-    take(4, last, 1)
     attend(4, last)
     finish(last)
     for which in range(2):

time: 59.7 us -> 59.7 us (level)
  no operation moved by 1% of the time
where the time goes in v3:
time: 59.7 us; the launch traced here: 59.6 us
  Pallas kernels  57.3 us (96%)
  local copies, waits for them, and re-layouts  2.3 us (4%)
    pallas_call x1, Pallas kernels, local(): pl.pallas_call(functools.partial(kernel, blocks), out_shape=jax.ShapeDtyp...  57.3 us
    unnamed x1, local copies, waits for them, and re-layouts  2.3 us

profile of v3, /device:TPU:17, one launch (start us, length us, event | category | flops | bytes accessed | tf_op | source)
XLA Modules:
  0.0 59.6 jit_solution(6981348873921366188)
XLA Ops:
  0.0 57.3 %shard_map.37 = bf16[256,2048]{1,0:T(8,128)(2,1)} custom-call(bf16[512,1024]{1,0:T(8,128)(2,1)} %q_hbm.1, bf16[512,512]{1,0:T(8,128)(2,1)} %k_hbm.1, bf16[512,512]{1,0:T(8,128)(2,1)} %v_hbm.1), custom_call_target="tpu_custom_call" | custom-call | tf_op jit(solution)/shard_map/pallas_call | solution.py:313
  57.3 2.3 %copy.5 = bf16[256,2048]{1,0:T(8,128)(2,1)} copy(bf16[256,2048]{1,0:T(8,128)(2,1)} %shard_map.37) | data formatting | bytes 2097152
